TPU v7x, 512 devices: a whole 4x8x8 slice. The times are simulated.
512 devices in a mesh: expert: 64 (over z, y_hi, x), tensor: 8 (over y_lo, core).
Axes of the slice: x: 4, y: 8 (y_hi: 2, y_lo: 4; y = y_hi * 4 + y_lo), z: 8, core: 2. Of those that a mesh axis runs over, the one named last changes fastest.
Arguments:
- grad_out: bfloat16 [8192, 4096], P('expert', 'tensor'), may hold values from -6 to 6
- dense_gate: bfloat16 [8192, 3072], P('expert', 'tensor'), may hold values from -6 to 6
- dense_up: bfloat16 [8192, 3072], P('expert', 'tensor'), may hold values from -6 to 6
- w_gate: bfloat16 [4096, 3072], P('expert', 'tensor'), may hold values from -0.109375 to 0.109375
- w_up: bfloat16 [4096, 3072], P('expert', 'tensor'), may hold values from -0.109375 to 0.109375
- w_down: bfloat16 [3072, 4096], P('tensor', 'expert'), may hold values from -0.09375 to 0.09375
- routes: int32 [8192, 2], P('expert'), may hold values from 0 to 63, all different within a row; in each aligned block of 128 rows (0 to 127, 128 to 255, ...) at most 5 rows name the same one
- route_weight: bfloat16 [8192, 2], P('expert'), may hold values from 0.25 to 1
- expert_down: bfloat16 [64, 3072, 4096], P('expert', 'tensor'), may hold values from -0.09375 to 0.09375
- expert_hidden: bfloat16 [64, 320, 3072], P('expert', None, 'tensor'), may hold values from -0.107910156 to 0.107910156
Outputs:
- input_grad: bfloat16 [8192, 4096], P('expert', 'tensor')
- hidden_grad: bfloat16 [64, 320, 3072], P('expert', None, 'tensor')
- route_grad: float32 [8192, 2], P('expert')
Inputs may be any that keep to these rules, and one draw needn't show every extreme that they name: `routes`: the two experts of a row differ. Among the rows of one index of expert (aligned blocks of 128 rows) no expert is named more than 5 times, a bound that some block reaches.
All inputs are finite; a program needn't handle non-finite values.
Results may differ from a plain program's by a relative error of at most 0.0049.
Values may be sent and summed in bfloat16 or wider, within the bound.
A program may use at most 64 MiB of HBM per device.

v0:
```python
import jax
import jax.numpy as jnp
from jax import lax
from jax.sharding import PartitionSpec as P


def contract_last(left, right):
    return lax.dot_general(
        left, right, (((1,), (1,)), ((), ())), preferred_element_type=jnp.float32
    )


def body(
    grad_out,
    dense_gate,
    dense_up,
    w_gate,
    w_up,
    w_down,
    routes,
    route_weight,
    expert_down,
    expert_hidden,
):
    whole_grad = lax.all_gather(grad_out, "tensor", axis=1, tiled=True)
    tok_count = whole_grad.shape[0]
    hidden_delta = contract_last(whole_grad, lax.all_gather(w_down, "expert", axis=1, tiled=True))
    gate_f = dense_gate.astype(jnp.float32)
    up_f = dense_up.astype(jnp.float32)
    sigmoid_gate = jax.nn.sigmoid(gate_f)
    swish_gate = gate_f * sigmoid_gate
    slope_gate = sigmoid_gate * (1.0 + gate_f * (1.0 - sigmoid_gate))
    gate_delta = (hidden_delta * up_f * slope_gate).astype(jnp.bfloat16)
    up_delta = (hidden_delta * swish_gate).astype(jnp.bfloat16)
    pieces = lax.all_gather((w_gate, w_up), "expert", axis=0, tiled=True)
    input_terms = contract_last(gate_delta, pieces[0]) + contract_last(up_delta, pieces[1])
    input_grad = lax.psum_scatter(input_terms, "tensor", scatter_dimension=1, tiled=True).astype(
        jnp.bfloat16
    )
    groups = lax.axis_size("expert")
    slot_count = expert_hidden.shape[1]
    capacity = slot_count // groups
    top_count = routes.shape[1]
    flat_routes = routes.reshape(-1)
    onehot = (flat_routes[:, None] == jnp.arange(groups, dtype=jnp.int32)[None, :]).astype(
        jnp.int32
    )
    earlier = jnp.cumsum(onehot, axis=0) - onehot
    slot_rank = jnp.sum(earlier * onehot, axis=1)
    target = flat_routes * capacity + slot_rank
    placed = jnp.arange(slot_count, dtype=jnp.int32)[:, None] == target[None, :]
    placed_half = placed.astype(jnp.bfloat16)
    token_map = jnp.sum(placed_half.reshape(slot_count, tok_count, top_count), axis=2)
    weight_sent = (
        jnp.dot(placed_half, route_weight.reshape(-1), preferred_element_type=jnp.float32)
        .astype(jnp.bfloat16)
        .reshape(groups, capacity)
    )
    expert_weight = expert_down[0]
    slice_sent = (
        jnp.dot(token_map, grad_out, preferred_element_type=jnp.float32)
        .astype(jnp.bfloat16)
        .reshape(groups, capacity, grad_out.shape[1])
    )
    slice_recv, slot_weight = (
        lax.all_to_all(slice_sent, "expert", split_axis=0, concat_axis=0, tiled=True),
        lax.all_to_all(weight_sent, "expert", split_axis=0, concat_axis=0, tiled=True),
    )
    slot_delta = contract_last(
        lax.all_gather(
            slice_recv.reshape(slot_count, grad_out.shape[1]), "tensor", axis=1, tiled=True
        ),
        expert_weight,
    )
    slot_weight = slot_weight.reshape(slot_count).astype(jnp.float32)
    hidden_grad = (slot_weight[:, None] * slot_delta).astype(jnp.bfloat16)[None]
    partial_value = jnp.sum(expert_hidden[0].astype(jnp.float32) * slot_delta, axis=1)
    placed_full = placed.astype(jnp.float32)
    returned = lax.all_to_all(
        partial_value.reshape(groups, capacity), "expert", split_axis=0, concat_axis=0, tiled=True
    )
    own_scores = jnp.dot(
        returned.reshape(-1), placed_full, precision=lax.Precision.HIGHEST
    ).reshape(tok_count, top_count)
    route_grad = lax.psum(own_scores, "tensor")
    return (input_grad, hidden_grad, route_grad)


def solution(mesh):
    in_specs = (
        P("expert", "tensor"),
        P("expert", "tensor"),
        P("expert", "tensor"),
        P("expert", "tensor"),
        P("expert", "tensor"),
        P("tensor", "expert"),
        P("expert", None),
        P("expert", None),
        P("expert", "tensor", None),
        P("expert", None, "tensor"),
    )
    out_specs = (P("expert", "tensor"), P("expert", None, "tensor"), P("expert", None))
    return jax.shard_map(body, mesh=mesh, in_specs=in_specs, out_specs=out_specs, check_vma=False)
```

profile of v0, /device:TPU:1, one launch (start us, length us, event | category | flops | bytes accessed | tf_op | source)
XLA Modules:
  0.0 593.9 jit_solution(17096740727562122995)
XLA Ops:
  7.2 0.0 copy-start
  7.2 0.0 all-gather.6.cloned.1.call-start
  7.2 0.7 all-gather.6.cloned.1.call-update
  7.9 0.0 all-gather.8.cloned.1.call-start
  8.0 0.7 all-gather.8.cloned.1.call-update
  8.7 0.0 all-gather.10.cloned.1.call-start
  8.7 0.7 all-gather.10.cloned.1.call-update
  9.4 0.0 all-gather.12.cloned.1.call-start
  9.4 0.5 all-gather.12.cloned.1.call-update
  10.0 0.0 all-gather.14.cloned.1.call-start
  10.0 0.8 copy.37
  10.8 0.1 eq.62
  10.9 0.1 reshape.102
  11.1 0.6 reduce-window.6
  11.7 0.2 slice_reduce_fusion
  11.9 0.1 fusion.24
  12.1 0.1 reduce_sum.33
  12.2 0.1 copy.42
  12.3 0.7 multiply_add_fusion
  13.0 1.1 convolution_convert_fusion
  14.2 0.9 reshape.105
  15.1 0.0 copy-start.1
  15.1 0.0 copy-start.2
  15.1 45.1 %all_to_all.24 = bf16[64,5,512]{2,1,0:T(8,128)(2,1)} all-to-all(bf16[64,5,512]{2,1,0:T(8,128)(2,1)} %reshape.105), channel_id=1, replica_groups=mesh['expert'=64,'tensor'=8] {'expert'}, dimensions={0} | all-to-all | bytes 655360 | tf_op jit(solution)/shard_map/all_to_all | solution.py:66
  60.2 1.9 reshape.106
  62.2 0.0 all-gather.14.cloned.1.call-update
  62.2 0.0 reduce-scatter.2.cloned.1.call-start
  62.2 0.0 all-gather.6.cloned.1.call-done
  62.3 140.9 %all-gather.8.cloned.1.call-done = bf16[384,4096]{0,1:T(8,128)(2,1)} async-done(((bf16[384,64]{0,1:T(8,128)(2,1)}), bf16[384,4096]{0,1:T(8,128)(2,1)}) %all-gather.8.cloned.1.call-update) | async-done | bytes 3145744 | tf_op jit(solution)/shard_map/all_gather | solution.py:27
  203.1 2.9 fusion.30
  206.1 141.0 %all-gather.10.cloned.1.call-done = bf16[4096,384]{1,0:T(8,128)(2,1)} async-done(((bf16[64,384]{1,0:T(8,128)(2,1)}), bf16[4096,384]{1,0:T(8,128)(2,1)}) %all-gather.10.cloned.1.call-update) | async-done | bytes 3145744 | tf_op jit(solution)/shard_map/all_gather | solution.py:35
  347.0 0.0 copy-done.1
  347.0 0.0 copy-done.2
  347.0 4.4 fusion.18
  351.4 0.0 copy-start.3
  351.4 139.4 %all-gather.12.cloned.1.call-done = bf16[4096,384]{1,0:T(8,128)(2,1)} async-done(((bf16[64,384]{1,0:T(8,128)(2,1)}), bf16[4096,384]{1,0:T(8,128)(2,1)}) %all-gather.12.cloned.1.call-update) | async-done | bytes 3145744 | tf_op jit(solution)/shard_map/all_gather | solution.py:35
  490.8 5.0 convolution_add_fusion
  495.8 0.0 reduce-scatter.2.cloned.1.call-update
  495.8 0.0 copy-done.3
  495.8 0.1 copy.40
  495.9 0.1 reshape.110
  496.1 0.2 convolution_reduce_fusion
  496.3 0.2 all_to_all.20
  496.5 18.4 %all_to_all.25 = bf16[64,1,5]{2,1,0:T(2,128)(2,1)S(1)} all-to-all(bf16[64,1,5]{2,1,0:T(2,128)(2,1)S(1)} %all_to_all.20), channel_id=1, replica_groups=mesh['expert'=64,'tensor'=8] {'expert'}, dimensions={0} | all-to-all | bytes 1280 | tf_op jit(solution)/shard_map/all_to_all | solution.py:67
  514.8 0.1 convert_reduce_fusion
  514.9 0.1 reshape.108
  515.1 19.8 %all-gather.14.cloned.1.call-done = bf16[320,4096]{1,0:T(8,128)(2,1)} async-done(((bf16[320,512]{1,0:T(8,128)(2,1)}), bf16[320,4096]{1,0:T(8,128)(2,1)}) %all-gather.14.cloned.1.call-update) | async-done | bytes 2621456 | tf_op jit(solution)/shard_map/all_gather | solution.py:70
  534.9 0.0 copy-done
  534.9 4.0 fusion.2
  538.8 0.8 all_to_all.18
  539.6 13.9 %all-to-all-start.2 = ((f32[64,1,5]{2,1,0:T(1,128)}), f32[64,1,5]{2,1,0:T(1,128)S(1)}, u32[]{:S(2)}, u32[]{:S(2)}) async-start(f32[64,1,5]{2,1,0:T(1,128)} %bitcast.5), calls=%async_computation.3 | async-start | bytes 65536 | tf_op jit(solution)/shard_map/all_to_all | solution.py:79
  553.6 0.1 iota_compare_fusion
  553.7 0.1 eq.74
  553.8 12.9 %all-to-all-done.2 = f32[64,1,5]{2,1,0:T(1,128)S(1)} async-done(((f32[64,1,5]{2,1,0:T(1,128)}), f32[64,1,5]{2,1,0:T(1,128)S(1)}, u32[]{:S(2)}, u32[]{:S(2)}) %all-to-all-start.2) | async-done | bytes 1312 | tf_op jit(solution)/shard_map/all_to_all | solution.py:79
  566.7 0.5 broadcast.64
  567.2 0.7 reduce.14
  568.0 0.1 reshape.107
  568.1 0.4 fusion.3
  568.5 0.1 copy.48
  568.5 16.9 %psum.7 = f32[128,2]{0,1:T(2,128)} all-reduce(f32[128,2]{0,1:T(2,128)S(1)} %copy.48), channel_id=1, replica_groups=mesh['expert'=64,'tensor'=8] {'tensor'}, use_global_device_ids=true, to_apply=%region_6.7 | all-reduce | flops 256 | bytes 2048 | tf_op jit(solution)/shard_map/psum | solution.py:85
  585.5 0.0 reduce-scatter.2.cloned.1.call-done
  585.5 1.6 convert_element_type.58
  (5 shorter events, 0.1 us)
Async XLA Ops:
  7.2 527.7 %copy-start = (bf16[1,384,4096]{2,1,0:T(8,128)(2,1)S(1)}, bf16[1,384,4096]{2,1,0:T(8,128)(2,1)}, u32[]{:S(2)}) copy-start(bf16[1,384,4096]{2,1,0:T(8,128)(2,1)} %param.18) | copy-start | bytes 9437188
  7.2 55.1 %all-gather.6.cloned.1.call-start = ((), (), s32[]{:S(2)}) async-start(), calls=%async_computation.4 | async-start | bytes 1179648 | tf_op jit(solution)/shard_map/all_gather | solution.py:25
  7.9 195.2 %all-gather.8.cloned.1.call-start = ((), (), s32[]{:S(2)}) async-start(), calls=%async_computation.5 | async-start | bytes 3194880 | tf_op jit(solution)/shard_map/all_gather | solution.py:27
  8.7 338.4 %all-gather.10.cloned.1.call-start = ((), (), s32[]{:S(2)}) async-start(), calls=%async_computation.6 | async-start | bytes 3194880 | tf_op jit(solution)/shard_map/all_gather | solution.py:35
  9.4 481.4 %all-gather.12.cloned.1.call-start = ((), (), s32[]{:S(2)}) async-start(), calls=%async_computation.7 | async-start | bytes 3194880 | tf_op jit(solution)/shard_map/all_gather | solution.py:35
  10.0 524.9 %all-gather.14.cloned.1.call-start = ((), (), s32[]{:S(2)}) async-start(), calls=%async_computation.9 | async-start | bytes 2949120 | tf_op jit(solution)/shard_map/all_gather | solution.py:70
  15.1 331.9 %copy-start.1 = (bf16[128,384]{1,0:T(8,128)(2,1)S(1)}, bf16[128,384]{1,0:T(8,128)(2,1)}, u32[]{:S(2)}) copy-start(bf16[128,384]{1,0:T(8,128)(2,1)} %param.11) | copy-start | bytes 294916
  15.1 331.9 %copy-start.2 = (bf16[128,384]{1,0:T(8,128)(2,1)S(1)}, bf16[128,384]{1,0:T(8,128)(2,1)}, u32[]{:S(2)}) copy-start(bf16[128,384]{1,0:T(8,128)(2,1)} %param.12) | copy-start | bytes 294916
  62.2 523.3 %reduce-scatter.2.cloned.1.call-start = ((), (), s32[]{:S(2)}) async-start(), calls=%async_computation.8 | async-start | bytes 2359296 | tf_op jit(solution)/shard_map/reduce_scatter | solution.py:37
  351.4 144.4 %copy-start.3 = (bf16[128,2]{0,1:T(2,128)(2,1)S(1)}, bf16[128,2]{0,1:T(2,128)(2,1)}, u32[]{:S(2)}) copy-start(bf16[128,2]{0,1:T(2,128)(2,1)} %param.17) | copy-start | bytes 1540
  539.6 27.1 %all-to-all-start.2 = ((f32[64,1,5]{2,1,0:T(1,128)}), f32[64,1,5]{2,1,0:T(1,128)S(1)}, u32[]{:S(2)}, u32[]{:S(2)}) async-start(f32[64,1,5]{2,1,0:T(1,128)} %bitcast.5), calls=%async_computation.3 | async-start | bytes 65536 | tf_op jit(solution)/shard_map/all_to_all | solution.py:79
Sparse Core Ops, SparseCore 0:
  10.1 46.7 all-gather.5
  61.4 141.7 all-gather.7
  207.7 139.3 all-gather.9
  351.4 139.3 all-gather.11
  492.7 42.1 all-gather.13
  537.6 42.8 reduce-scatter.1
where the time goes:
time: 594 us
  waiting for transfers between devices  457 us (77%)
  blocking collectives  80.5 us (14%)
  matrix products  17.6 us (3%)
  starting transfers between devices  14.2 us (2%)
  between operations  14.2 us (2%)
  local copies, waits for them, and re-layouts  6.5 us (1%)
    all_gather x2, waiting for transfers between devices, body(): pieces = lax.all_gather((w_gate, w_up), 'expert', axis=0, tiled=True)  280 us
    all_gather x1, waiting for transfers between devices, body(): lax.all_gather(w_down, 'expert', axis=1, tiled=True)  141 us
    all_to_all x1, blocking collectives, body(): lax.all_to_all(slice_sent, 'expert', split_axis=0, concat_axis=0, tiled=T...  45.1 us
    all_gather x1, waiting for transfers between devices, body(): lax.all_gather(slice_recv.reshape(slot_count, grad_out.shape[1]), 'tensor...  19.8 us
    all_to_all x1, blocking collectives, body(): lax.all_to_all(weight_sent, 'expert', split_axis=0, concat_axis=0, tiled=...  18.4 us
    psum x1, blocking collectives, body(): route_grad = lax.psum(own_scores, 'tensor')  16.9 us
    dot_general x4, matrix products, contract_last(): lax.dot_general(left, right, (((1,), (1,)), ((), ())), preferred_element_...  16.3 us
    all_to_all x1, starting transfers between devices, body(): lax.all_to_all(partial_value.reshape(groups, capacity), 'expert', split_a...  13.9 us
  transfers between devices with their start and end apart: 7, of which 5 were waited for; matrix products, arithmetic and copies ran while one was open for 4% of the time, Pallas kernels for 0%

commit v1 on v0

v1 whole, which is shorter than its diff:
```python
import jax
import jax.numpy as jnp
import numpy as np
from jax import lax
from jax.experimental import pallas as pl
from jax.experimental.pallas import tpu as pltpu
from jax.sharding import PartitionSpec as P

MESH = pl.DeviceIdType.MESH
F32 = jnp.float32
BF16 = jnp.bfloat16
CAP = 5
BLK = 48
N_COPY = 160


def dot_nt(a, b):
    return lax.dot_general(a, b, (((1,), (1,)), ((), ())), preferred_element_type=F32)


def dot_tn(a, b):
    return lax.dot_general(a, b, (((0,), (0,)), ((), ())), preferred_element_type=F32)


def dot_nn(a, b):
    return jnp.dot(a, b, preferred_element_type=F32)


def tables():
    p2 = np.zeros((8 * BLK, 8 * BLK), np.float32)
    p3 = np.zeros((320, 8 * BLK), np.float32)
    p4 = np.zeros((320, 8 * BLK), np.float32)
    m5 = np.zeros((320, 128), np.float32)
    for j in range(8):
        for z in range(8):
            p2[j * BLK + 40 + z, z * BLK + 40 + j] = 1
            for s in range(CAP):
                p2[j * BLK + z * CAP + s, z * BLK + j * CAP + s] = 1
                row = z * 40 + j * CAP + s
                p3[row, j * BLK + z * CAP + s] = 1
                p4[row, j * BLK + 40 + z] = 1
                m5[row, s] = 1
    return p2, p3, p4, m5


def kernel(
    grad, gate, up, wd, wg, wu, routes, rw, ed_hbm, hid, p2, p3, p4, m5,
    out_g, out_h, out_r,
    W, G, SL, S1, R1, S2, R2, ED, acc, K, XS, XR, YS, YR, RT0, RT1, ST2, RT2,
    ssem, rsem, lsem, ysend, yrecv,
):
    e = lax.axis_index("expert")
    t = lax.axis_index("tensor")
    z = e // 8
    j = lax.rem(e, 8)
    yh = j // 4
    x = lax.rem(j, 4)
    yl = t // 2
    c = lax.rem(t, 2)
    yo = 1 - yh

    def zz(d):
        return lax.rem(z + d + 8, 8)

    def xx(d):
        return lax.rem(x + d, 4)

    def z_dev(d):
        return (zz(d) * 8 + j, t)

    def x_dev(d):
        return (z * 8 + yh * 4 + xx(d), t)

    def j_dev(d):
        return (z * 8 + lax.rem(j + d, 8), t)

    y_dev = (z * 8 + yo * 4 + x, t)
    sibling = (e, yl * 2 + 1 - c)

    def yl_dev(d):
        return (e, lax.rem(yl + d, 4) * 2 + c)

    def t_dev(d):
        return (e, lax.rem(t + d, 8))

    barrier = pltpu.get_barrier_semaphore()
    for d in range(1, 8):
        for dev in (z_dev(d), j_dev(d), t_dev(d)):
            pl.semaphore_signal(barrier, inc=1, device_id=dev, device_id_type=MESH)

    ed_copy = pltpu.make_async_copy(ed_hbm, ED, lsem)
    ed_copy.start()

    count = [0]
    sends = []

    def send(src, dst, dev):
        i = count[0]
        count[0] += 1
        copy = pltpu.make_async_remote_copy(
            src_ref=src, dst_ref=dst, send_sem=ssem.at[i], recv_sem=rsem.at[i],
            device_id=dev, device_id_type=MESH,
        )
        copy.start()
        sends.append(copy)
        return copy

    W[0, z, yh, x] = wd[...]
    W[1, z, yh, x] = wg[...]
    W[2, z, yh, x] = wu[...]
    G[t] = grad[...]

    lane = lax.broadcasted_iota(jnp.int32, (128, 128), 1).astype(F32)
    row = lax.broadcasted_iota(jnp.int32, (128, 128), 0).astype(F32)
    lane_b = lax.broadcasted_iota(jnp.int32, (128, 8 * BLK), 1).astype(F32)
    route = [routes[:, k : k + 1] for k in range(2)]
    onehot = [(route[k].astype(F32) == lane).astype(F32) for k in range(2)]
    lower = (lane < row).astype(BF16)
    earlier = dot_nn(lower, (onehot[0] + onehot[1]).astype(BF16))
    rank = [
        jnp.sum(earlier * onehot[0], axis=1, keepdims=True),
        jnp.sum((earlier + onehot[0]) * onehot[1], axis=1, keepdims=True),
    ]
    slot_map = jnp.zeros((128, 8 * BLK), F32)
    weight_rows = jnp.zeros((8 * BLK, 128), F32)
    for k in range(2):
        base = (lax.shift_right_logical(route[k], 3) * BLK).astype(F32)
        low = lax.bitwise_and(route[k], 7).astype(F32)
        slot_map += (base + low * CAP + rank[k] == lane_b).astype(F32)
        spare = (base + low + 40.0 == lane_b).astype(BF16)
        value = jnp.where(lane == rank[k], rw[:, k : k + 1].astype(F32), 0.0).astype(BF16)
        weight_rows += dot_tn(spare, value)
    filled = dot_tn(slot_map.astype(BF16), grad[...])
    first = (filled[:, 0:128] + weight_rows).astype(BF16)
    for k in range(8):
        S1[k, :, 0:128] = first[k * BLK : (k + 1) * BLK]
        S1[k, :, 128:512] = filled[k * BLK : (k + 1) * BLK, 128:512].astype(BF16)
    R1[z] = S1[z]

    pl.semaphore_wait(barrier, 21)

    disp1 = [send(S1.at[zz(d)], R1.at[z], z_dev(d)) for d in range(1, 8)]

    kinds = (pl.ds(0, 1), pl.ds(1, 2))

    def a_ring(kd, step, right):
        sign = 1 if right else -1
        zc = zz(-sign * (step - 1))
        ref = W.at[kinds[kd], zc, yh, x]
        if step == 4:
            ref = W.at[kinds[kd], zc, yh, x, pl.ds(0 if right else 32, 32)]
        return send(ref, ref, z_dev(sign))

    def b_ring(kd, step, right):
        sign = 1 if right else -1
        zc = zz(-sign * (step - 1))
        ref = W.at[kinds[kd], zc, yo]
        if step == 4:
            ref = W.at[kinds[kd], zc, yo, pl.ds(0 if right else 2, 2)]
        return send(ref, ref, z_dev(sign))

    def x_send(kd, delta, half):
        ref = W.at[kinds[kd], zz(delta), half, x]
        return [send(ref, ref, x_dev(d)) for d in range(1, 4)]

    def gather_start(buf):
        own = buf.at[t]
        return [send(own, own, yl_dev(d)) for d in range(1, 4)] + [send(own, own, sibling)]

    def gather_forward(buf, first_copies):
        out = []
        for d in range(1, 4):
            first_copies[d - 1].wait_recv()
            ref = buf.at[lax.rem(yl - d + 4, 4) * 2 + c]
            out.append(send(ref, ref, sibling))
        return out

    a = {}
    b = {}
    ax = {}
    for kd in range(2):
        ref = W.at[kinds[kd], z, yh, x]
        for right in (True, False):
            a[kd, 1, right] = a_ring(kd, 1, right)
        a[kd, 0] = send(ref, ref, y_dev)
        if kd == 0:
            tok = gather_start(G)
        ax[kd, 0] = x_send(kd, 0, yh)

    def a_step(kd, step):
        a[kd, step, True].wait_recv()
        if step < 4:
            a[kd, step + 1, True] = a_ring(kd, step + 1, True)
        a[kd, step, False].wait_recv()
        if step < 4:
            a[kd, step + 1, False] = a_ring(kd, step + 1, False)
            ax[kd, -step] = x_send(kd, -step, yh)
            ax[kd, step] = x_send(kd, step, yh)
        else:
            ax[kd, 4] = x_send(kd, 4, yh)

    def b_step(kd, step):
        b[kd, step, True].wait_recv()
        if step < 4:
            b[kd, step + 1, True] = b_ring(kd, step + 1, True)
        b[kd, step, False].wait_recv()
        if step < 4:
            b[kd, step + 1, False] = b_ring(kd, step + 1, False)

    bx = {}

    def b_open(kd):
        for copy in bx[kd]:
            copy.wait_recv()
        for right in (True, False):
            b[kd, 1, right] = b_ring(kd, 1, right)

    a_step(0, 1)
    a[0, 0].wait_recv()
    bx[0] = x_send(0, 0, yo)
    for copy in disp1:
        copy.wait_recv()
    shuffled = dot_nn(p2[...], R1[...].reshape(8 * BLK, 512)).astype(BF16)
    S2[...] = shuffled.reshape(8, BLK, 512)
    R2[j] = S2[j]
    disp2 = [send(S2.at[lax.rem(j + d, 8)], R2.at[j], j_dev(d)) for d in range(1, 8)]

    a_step(1, 1)
    a[1, 0].wait_recv()
    bx[1] = x_send(1, 0, yo)
    tok_fwd = gather_forward(G, tok)
    a_step(0, 2)
    b_open(0)
    a_step(1, 2)
    b_open(1)

    for copy in disp2:
        copy.wait_recv()
    arrived = R2[...].reshape(8 * BLK, 512)
    SL[t] = dot_nn(p3[...], arrived).astype(BF16)
    slots = gather_start(SL)
    slot_weight = jnp.sum(dot_nn(p4[...], arrived[:, 0:128]) * m5[...], axis=1, keepdims=True)

    a_step(0, 3)
    b_step(0, 1)
    a_step(1, 3)
    a_step(0, 4)
    b_step(0, 2)
    a_step(1, 4)
    b_step(1, 1)
    b_step(0, 3)
    b_step(0, 4)

    tok[3].wait_recv()
    for copy in tok_fwd:
        copy.wait_recv()
    for delta in (0, -1, 1, -2, 2, -3, 3, 4):
        for copy in ax[0, delta]:
            copy.wait_recv()
    hd = jnp.zeros((128, 384), F32)
    for k in range(8):
        hd += dot_nn(G[k], W[0, k].reshape(512, 384))
    gate_f = gate[...].astype(F32)
    up_f = up[...].astype(F32)
    sig = jax.nn.sigmoid(gate_f)
    swish = gate_f * sig
    slope = sig * (1.0 + gate_f * (1.0 - sig))
    gd = (hd * up_f * slope).astype(BF16)
    ud = (hd * swish).astype(BF16)

    b_step(1, 2)

    slots_fwd = gather_forward(SL, slots)
    ed_copy.wait()

    def expert_term(idx):
        cols = pl.ds(pl.multiple_of(idx * 512, 512), 512)
        return dot_nt(SL[idx], ED[:, cols])

    acc[...] = expert_term(t)
    for d in range(1, 4):
        acc[...] += expert_term(lax.rem(yl - d + 4, 4) * 2 + c)
    slots[3].wait_recv()
    acc[...] += expert_term(yl * 2 + 1 - c)
    for d in range(1, 4):
        slots_fwd[d - 1].wait_recv()
        acc[...] += expert_term(lax.rem(yl - d + 4, 4) * 2 + 1 - c)
    out_h[...] = (slot_weight * acc[...]).astype(BF16)
    part = jnp.sum(hid[...].astype(F32) * acc[...], axis=1, keepdims=True)
    diag = lax.broadcasted_iota(jnp.int32, (40, 128), 0) == lax.broadcasted_iota(
        jnp.int32, (40, 128), 1
    )
    tile = jnp.concatenate(
        [
            jnp.sum(jnp.where(diag, part[k * 40 : (k + 1) * 40], 0.0), axis=0, keepdims=True)
            for k in range(8)
        ],
        axis=0,
    )
    RT0[t] = tile
    own = RT0.at[t]
    ret0 = [send(own, own, t_dev(d)) for d in range(1, 8)]

    b_step(1, 3)

    for copy in ret0:
        copy.wait_recv()
    RT1[j] = jnp.sum(RT0[...], axis=0)
    own1 = RT1.at[j]
    ret1 = [send(own1, own1, j_dev(d)) for d in range(1, 8)]

    def pair(q):
        def block(zb):
            return dot_nt(gd, W[1, zb].reshape(512, 384)) + dot_nt(ud, W[2, zb].reshape(512, 384))

        XS[q] = block(2 * q + 1 - c).astype(BF16)
        copy = send(XS.at[q], XR.at[q], sibling)
        K[q] = block(2 * q + c)
        return copy

    def y_copy(q, src):
        return pltpu.make_async_remote_copy(
            src_ref=YS.at[q], dst_ref=YR.at[src], send_sem=ysend.at[q], recv_sem=yrecv.at[src],
            device_id=(e, q * 2 + c), device_id_type=MESH,
        )

    def pass_on(q, copy):
        copy.wait_recv()
        K[q] = K[q] + XR[q].astype(F32)

        @pl.when(q != yl)
        def _():
            YS[q] = K[q].astype(BF16)
            y_copy(q, yl).start()

    def x_wait(delta):
        for copy in ax[1, delta]:
            copy.wait_recv()

    zq = z // 2

    def qq(d):
        return lax.rem(zq + d, 4)

    for delta in (0, -1, 1):
        x_wait(delta)
    p0 = pair(qq(0))

    for copy in ret1:
        copy.wait_recv()
    for k in range(8):
        ST2[k] = RT1[:, k, :]
    RT2[z] = ST2[z]
    ret2 = [send(ST2.at[zz(d)], RT2.at[z], z_dev(d)) for d in range(1, 8)]

    pass_on(qq(0), p0)
    for delta in (-2, 2, -3, 3):
        x_wait(delta)
    p1 = pair(qq(3))
    p2_ = pair(qq(1))
    pass_on(qq(3), p1)
    pass_on(qq(1), p2_)
    b_step(1, 4)
    x_wait(4)
    p3_ = pair(qq(2))

    for copy in ret2:
        copy.wait_recv()
    back = RT2[...].reshape(64, 128)
    jf = (j * CAP).astype(F32)
    for k in range(2):
        scores = jnp.dot(
            onehot[k][:, 0:64], back, preferred_element_type=F32, precision=lax.Precision.HIGHEST
        )
        out_r[:, k : k + 1] = jnp.sum(
            jnp.where(lane == rank[k] + jf, scores, 0.0), axis=1, keepdims=True
        )

    pass_on(qq(2), p3_)
    total = K[yl]
    for d in range(1, 4):
        src = lax.rem(yl + d, 4)
        y_copy(src, src).wait_recv()
        total += YR[src].astype(F32)
    out_g[...] = total.astype(BF16)
    for d in range(1, 4):
        q = lax.rem(yl + d, 4)
        y_copy(q, q).wait_send()
    for copy in sends:
        copy.wait_send()


def body(
    grad_out, dense_gate, dense_up, w_gate, w_up, w_down, routes, route_weight,
    expert_down, expert_hidden,
):
    p2, p3, p4, m5 = tables()
    vmem = pl.BlockSpec(memory_space=pltpu.VMEM)
    hbm = pl.BlockSpec(memory_space=pl.ANY)
    out_g, out_h, out_r = pl.pallas_call(
        kernel,
        out_shape=(
            jax.ShapeDtypeStruct((128, 512), BF16),
            jax.ShapeDtypeStruct((320, 384), BF16),
            jax.ShapeDtypeStruct((128, 2), F32),
        ),
        in_specs=[vmem] * 8 + [hbm] + [vmem] * 5,
        out_specs=(vmem, vmem, vmem),
        scratch_shapes=[
            pltpu.VMEM((3, 8, 2, 4, 64, 384), BF16),
            pltpu.VMEM((8, 128, 512), BF16),
            pltpu.VMEM((8, 320, 512), BF16),
            pltpu.VMEM((8, BLK, 512), BF16),
            pltpu.VMEM((8, BLK, 512), BF16),
            pltpu.VMEM((8, BLK, 512), BF16),
            pltpu.VMEM((8, BLK, 512), BF16),
            pltpu.VMEM((384, 4096), BF16),
            pltpu.VMEM((320, 384), F32),
            pltpu.VMEM((4, 128, 512), F32),
            pltpu.VMEM((4, 128, 512), BF16),
            pltpu.VMEM((4, 128, 512), BF16),
            pltpu.VMEM((4, 128, 512), BF16),
            pltpu.VMEM((4, 128, 512), BF16),
            pltpu.VMEM((8, 8, 128), F32),
            pltpu.VMEM((8, 8, 128), F32),
            pltpu.VMEM((8, 8, 128), F32),
            pltpu.VMEM((8, 8, 128), F32),
            pltpu.SemaphoreType.DMA((N_COPY,)),
            pltpu.SemaphoreType.DMA((N_COPY,)),
            pltpu.SemaphoreType.DMA,
            pltpu.SemaphoreType.DMA((4,)),
            pltpu.SemaphoreType.DMA((4,)),
        ],
        compiler_params=pltpu.CompilerParams(
            collective_id=0, has_side_effects=True, vmem_limit_bytes=48 << 20
        ),
    )(
        grad_out, dense_gate, dense_up, w_down.T, w_gate, w_up, routes, route_weight,
        expert_down[0], expert_hidden[0],
        jnp.asarray(p2, BF16), jnp.asarray(p3, BF16), jnp.asarray(p4, BF16), jnp.asarray(m5, F32),
    )
    return out_g, out_h[None], out_r


def solution(mesh):
    in_specs = (
        P("expert", "tensor"),
        P("expert", "tensor"),
        P("expert", "tensor"),
        P("expert", "tensor"),
        P("expert", "tensor"),
        P("tensor", "expert"),
        P("expert", None),
        P("expert", None),
        P("expert", "tensor", None),
        P("expert", None, "tensor"),
    )
    out_specs = (P("expert", "tensor"), P("expert", None, "tensor"), P("expert", None))
    return jax.shard_map(body, mesh=mesh, in_specs=in_specs, out_specs=out_specs, check_vma=False)
```

time: 594 us -> 131 us (0.22)
  the two profiles are of different devices: /device:TPU:1 before, /device:TPU:48 now
where the time goes in v1:
time: 131 us
  Pallas kernels  115 us (88%)
  local copies, waits for them, and re-layouts  15.2 us (12%)
    pallas_call x1, Pallas kernels, body(): pl.pallas_call(kernel, out_shape=(jax.ShapeDtypeStruct((128, 512), BF16),...  115 us
    unnamed x29, local copies, waits for them, and re-layouts  15.2 us

profile of v1, /device:TPU:48, one launch (start us, length us, event | category | flops | bytes accessed | tf_op | source)
XLA Modules:
  0.0 130.5 jit_solution(9348245634343251888)
XLA Ops:
  0.6 0.8 copy.18.rw
  1.4 0.8 copy.17.routes
  2.2 0.0 copy-start
  2.2 1.9 %copy-done = bf16[1,384,4096]{2,1,0:T(8,128)(2,1)S(1)} copy-done((bf16[1,384,4096]{2,1,0:T(8,128)(2,1)S(1)}, bf16[1,384,4096]{2,1,0:T(8,128)(2,1)}, u32[]{:S(2)}) %copy-start) | copy-done | bytes 3145752
  4.1 0.0 copy-start.1
  4.1 1.0 copy-done.1
  5.1 0.0 copy-start.2
  5.1 0.9 copy-done.2
  6.0 0.0 copy-start.3
  6.0 0.9 copy-done.3
  6.9 0.0 copy-start.4
  6.9 0.9 copy-done.4
  7.9 0.0 copy-start.5
  7.9 0.9 copy-done.5
  8.8 0.0 copy-start.6
  8.8 0.9 copy-done.6
  9.7 0.0 copy-start.7
  9.7 0.9 copy-done.7
  10.6 0.0 copy-start.8
  10.6 0.9 copy-done.8
  11.5 0.0 copy-start.9
  11.5 0.8 copy-done.9
  12.3 0.0 copy-start.10
  12.3 0.8 copy-done.10
  13.1 0.0 copy-start.11
  13.1 0.8 copy-done.11
  13.9 114.6 %shard_map.157 = (bf16[128,512]{1,0:T(8,128)(2,1)S(1)}, bf16[320,384]{1,0:T(8,128)(2,1)S(1)}, f32[128,2]{1,0:T(8,128)S(1)}) custom-call(bf16[128,512]{1,0:T(8,128)(2,1)S(1)} %copy-done.6, bf16[128,384]{1,0:T(8,128)(2,1)S(1)} %copy-done.7, bf16[128,384]{1,0:T(8,128)(2,1)S(1)} %copy-done.8, bf16[64,384]{1,0:T(8,128)(2,1)S(1)} %bitcast.7, ...), custom_call_target="tpu_custom_call" | custom-call | tf_op jit(solution)/shard_map/pallas_call | solution.py:400
  128.5 0.6 copy.19
  129.2 0.7 copy.22
  129.8 0.7 copy.23
Async XLA Ops:
  2.2 1.9 %copy-start = (bf16[1,384,4096]{2,1,0:T(8,128)(2,1)S(1)}, bf16[1,384,4096]{2,1,0:T(8,128)(2,1)}, u32[]{:S(2)}) copy-start(bf16[1,384,4096]{2,1,0:T(8,128)(2,1)} %param.22) | copy-start | bytes 9437188
  4.1 1.0 copy-start.1
  5.1 0.9 copy-start.2
  6.0 0.9 copy-start.3
  6.9 0.9 copy-start.4
  7.9 0.9 copy-start.5
  8.8 0.9 copy-start.6
  9.7 0.9 copy-start.7
  10.6 0.9 copy-start.8
  11.5 0.8 copy-start.9
  12.3 0.8 copy-start.10
  13.1 0.8 copy-start.11

commit v2 on v1

v2 whole, which is shorter than its diff:
```python
import jax
import jax.numpy as jnp
import numpy as np
from jax import lax
from jax.experimental import pallas as pl
from jax.experimental.pallas import tpu as pltpu
from jax.sharding import PartitionSpec as P

MESH = pl.DeviceIdType.MESH
F32 = jnp.float32
BF16 = jnp.bfloat16
CAP = 5
BLK = 48
N_COPY = 160


def dot_nt(a, b):
    return lax.dot_general(a, b, (((1,), (1,)), ((), ())), preferred_element_type=F32)


def dot_tn(a, b):
    return lax.dot_general(a, b, (((0,), (0,)), ((), ())), preferred_element_type=F32)


def dot_nn(a, b):
    return jnp.dot(a, b, preferred_element_type=F32)


def tables():
    p2 = np.zeros((8 * BLK, 8 * BLK), np.float32)
    p3 = np.zeros((320, 8 * BLK), np.float32)
    p4 = np.zeros((64, 8 * BLK), np.float32)
    p5 = np.zeros((320, 128), np.float32)
    m5 = np.zeros((320, 128), np.float32)
    for h in range(2):
        for x in range(4):
            for z in range(8):
                j = h * 4 + x
                p2[x * 96 + 80 + h * 8 + z, z * BLK + 40 + j] = 1
                p4[h * 32 + z * 4 + x, x * 96 + 80 + h * 8 + z] = 1
                for s in range(CAP):
                    p2[x * 96 + h * 40 + z * CAP + s, z * BLK + j * CAP + s] = 1
                    p3[h * 160 + z * 20 + x * CAP + s, x * 96 + h * 40 + z * CAP + s] = 1
                    row = z * 40 + j * CAP + s
                    p5[row, h * 32 + z * 4 + x] = 1
                    m5[row, s] = 1
    return p2, p3, p4, p5, m5


def kernel(
    rw, grad_in, gate_in, up_in, wd_in, wg_in, wu_in, routes_in, ed_in, hid_in,
    p2_in, p3_in, p4_in, p5_in, m5_in,
    out_g, out_h, out_r,
    gate, up, routes, hid, p2, p3, p4, p5, m5,
    W, G, SL, S1, R1, S2, R2, DB, WR, WX, ED, half_acc, acc, K, XS, XR, YS, YR, RT0, RT1, ST2, RT2,
    ssem, rsem, lsem, xsend, xrecv, ysend, yrecv,
):
    e = lax.axis_index("expert")
    t = lax.axis_index("tensor")
    z = e // 8
    j = lax.rem(e, 8)
    yh = j // 4
    x = lax.rem(j, 4)
    yl = t // 2
    c = lax.rem(t, 2)
    yo = 1 - yh

    def zz(d):
        return lax.rem(z + d + 8, 8)

    def xx(d):
        return lax.rem(x + d, 4)

    def z_dev(d):
        return (zz(d) * 8 + j, t)

    def x_dev(d):
        return (z * 8 + yh * 4 + xx(d), t)

    def j_dev(d):
        return (z * 8 + lax.rem(j + d, 8), t)

    y_dev = (z * 8 + yo * 4 + x, t)
    sibling = (e, yl * 2 + 1 - c)

    def yl_dev(d):
        return (e, lax.rem(yl + d, 4) * 2 + c)

    def t_dev(d):
        return (e, lax.rem(t + d, 8))

    def far_dev(d):
        return (z * 8 + yo * 4 + x, lax.rem(yl + d, 4) * 2 + c)

    barrier = pltpu.get_barrier_semaphore()
    for d in range(1, 8):
        for dev in (z_dev(d), j_dev(d), t_dev(d)):
            pl.semaphore_signal(barrier, inc=1, device_id=dev, device_id_type=MESH)
    for d in range(1, 4):
        pl.semaphore_signal(barrier, inc=1, device_id=far_dev(d), device_id_type=MESH)

    local = {}

    def fetch(name, src, dst):
        copy = pltpu.make_async_copy(src, dst, lsem.at[len(local)])
        copy.start()
        local[name] = copy

    fetch("wd", wd_in, W.at[0, z, yh, x])
    fetch("wg", wg_in, W.at[1, z, yh, x])
    fetch("wu", wu_in, W.at[2, z, yh, x])
    fetch("grad", grad_in, G.at[t])
    fetch("routes", routes_in, routes)
    fetch("p2", p2_in, p2)
    fetch("p3", p3_in, p3)
    fetch("p4", p4_in, p4)
    fetch("p5", p5_in, p5)
    fetch("m5", m5_in, m5)
    fetch("gate", gate_in, gate)
    fetch("up", up_in, up)
    fetch("hid", hid_in, hid)
    fetch("ed", ed_in, ED)

    count = [0]
    sends = []

    def send(src, dst, dev):
        i = count[0]
        count[0] += 1
        copy = pltpu.make_async_remote_copy(
            src_ref=src, dst_ref=dst, send_sem=ssem.at[i], recv_sem=rsem.at[i],
            device_id=dev, device_id_type=MESH,
        )
        copy.start()
        sends.append(copy)
        return copy

    kinds = (pl.ds(0, 1), pl.ds(1, 2))

    def ring(kd, half, step, right):
        sign = 1 if right else -1
        zc = zz(-sign * (step - 1))
        if half == "own":
            ref = W.at[kinds[kd], zc, yh]
            if step == 4:
                ref = W.at[kinds[kd], zc, yh, pl.ds(0 if right else 2, 2)]
        else:
            ref = W.at[kinds[kd], zc, yo, x]
            if step == 4:
                ref = W.at[kinds[kd], zc, yo, x, pl.ds(0 if right else 32, 32)]
        return send(ref, ref, z_dev(sign))

    def x_send(kd, delta, half):
        ref = W.at[kinds[kd], zz(delta), half, x]
        return [send(ref, ref, x_dev(d)) for d in range(1, 4)]

    def gather_start(buf):
        own = buf.at[t]
        return [send(own, own, yl_dev(d)) for d in range(1, 4)] + [send(own, own, sibling)]

    def gather_forward(buf, first_copies):
        out = []
        for d in range(1, 4):
            first_copies[d - 1].wait_recv()
            ref = buf.at[lax.rem(yl - d + 4, 4) * 2 + c]
            out.append(send(ref, ref, sibling))
        return out

    a = {}
    b = {}
    ax = {}
    bx = {}

    def a_open(kd):
        across[kd].wait_recv()
        for right in (True, False):
            a[kd, 1, right] = ring(kd, "other", 1, right)
        ax[kd, 0] = x_send(kd, 0, yo)

    def a_step(kd, step):
        a[kd, step, True].wait_recv()
        if step < 4:
            a[kd, step + 1, True] = ring(kd, "other", step + 1, True)
        a[kd, step, False].wait_recv()
        if step < 4:
            a[kd, step + 1, False] = ring(kd, "other", step + 1, False)
            ax[kd, -step] = x_send(kd, -step, yo)
            ax[kd, step] = x_send(kd, step, yo)
        else:
            ax[kd, 4] = x_send(kd, 4, yo)

    def b_open(kd):
        for copy in bx[kd]:
            copy.wait_recv()
        for right in (True, False):
            b[kd, 1, right] = ring(kd, "own", 1, right)

    def b_step(kd, step):
        b[kd, step, True].wait_recv()
        if step < 4:
            b[kd, step + 1, True] = ring(kd, "own", step + 1, True)
        b[kd, step, False].wait_recv()
        if step < 4:
            b[kd, step + 1, False] = ring(kd, "own", step + 1, False)

    lane = lax.broadcasted_iota(jnp.int32, (128, 128), 1).astype(F32)
    row = lax.broadcasted_iota(jnp.int32, (128, 128), 0).astype(F32)
    lane_b = lax.broadcasted_iota(jnp.int32, (128, 8 * BLK), 1).astype(F32)
    local["routes"].wait()

    def column(values):
        return jnp.sum(jnp.where(lane == row, values, 0.0), axis=1, keepdims=True)

    high = [lax.shift_right_logical(routes[k : k + 1, :], 3) for k in range(2)]
    low = [lax.bitwise_and(routes[k : k + 1, :], 7) for k in range(2)]
    base = [column((high[k] * BLK + low[k] * CAP).astype(F32)) for k in range(2)]
    spare = [column((high[k] * BLK + low[k] + 40).astype(F32)) for k in range(2)]
    onehot = [(column(routes[k : k + 1, :].astype(F32)) == lane).astype(F32) for k in range(2)]
    lower = (lane < row).astype(BF16)
    earlier = dot_nn(lower, (onehot[0] + onehot[1]).astype(BF16))
    rank = [
        jnp.sum(earlier * onehot[0], axis=1, keepdims=True),
        jnp.sum((earlier + onehot[0]) * onehot[1], axis=1, keepdims=True),
    ]
    slot_map = jnp.zeros((128, 8 * BLK), F32)
    weight_rows = jnp.zeros((8 * BLK, 128), F32)
    for k in range(2):
        slot_map += (base[k] + rank[k] == lane_b).astype(F32)
        weight = column(rw[k : k + 1, :].astype(F32))
        value = jnp.where(lane == rank[k], weight, 0.0).astype(BF16)
        weight_rows += dot_tn((spare[k] == lane_b).astype(BF16), value)
    local["grad"].wait()
    filled = dot_tn(slot_map.astype(BF16), G[t])
    first = (filled[:, 0:128] + weight_rows).astype(BF16)
    for k in range(8):
        S1[k, :, 0:128] = first[k * BLK : (k + 1) * BLK]
        S1[k, :, 128:512] = filled[k * BLK : (k + 1) * BLK, 128:512].astype(BF16)
    R1[z] = S1[z]

    pl.semaphore_wait(barrier, 24)
    disp1 = [send(S1.at[zz(d)], R1.at[z], z_dev(d)) for d in range(1, 8)]
    local["wd"].wait()
    local["wg"].wait()
    local["wu"].wait()
    across = {}
    for kd in range(2):
        ref = W.at[kinds[kd], z, yh, x]
        bx[kd] = x_send(kd, 0, yh)
        across[kd] = send(ref, ref, y_dev)
    tok = gather_start(G)
    local["p2"].wait()
    for copy in disp1:
        copy.wait_recv()
    shuffled = dot_nn(p2[...], R1[...].reshape(8 * BLK, 512)).astype(BF16)
    S2[...] = shuffled.reshape(4, 96, 512)
    R2[x] = S2[x]
    disp2 = [send(S2.at[xx(d)], R2.at[x], x_dev(d)) for d in range(1, 4)]
    b_open(0)
    b_open(1)

    a_open(0)
    b_step(0, 1)
    a_open(1)
    a_step(0, 1)
    tok_fwd = gather_forward(G, tok)

    a_step(1, 1)
    for name in ("p3", "p4", "p5", "m5"):
        local[name].wait()
    for copy in disp2:
        copy.wait_recv()
    arrived = R2[...].reshape(8 * BLK, 512)
    DB[...] = dot_nn(p3[...], arrived).astype(BF16).reshape(2, 160, 512)
    WR[...] = dot_nn(p4[...], arrived[:, 0:128]).astype(BF16).reshape(2, 32, 128)
    SL[yh, t] = DB[yh]
    mine = SL.at[yh, t]
    near = [send(mine, mine, yl_dev(d)) for d in range(1, 4)]
    far = [send(DB.at[yo], mine, far_dev(d)) for d in range(4)]
    twin = [send(mine, mine, sibling)]
    weights_far = send(WR.at[yo], WX, y_dev)
    sends.pop()

    b_step(0, 2)
    a_step(0, 2)
    b_step(1, 1)
    a_step(1, 2)
    b_step(0, 3)
    a_step(0, 3)
    a_step(1, 3)
    a_step(0, 4)
    b_step(0, 4)
    a_step(1, 4)
    b_step(1, 2)

    for name in ("hid", "ed"):
        local[name].wait()
    def expert_term(h, idx):
        cols = pl.ds(pl.multiple_of(idx * 512, 512), 512)
        return dot_nt(SL[h, idx], ED[:, cols])

    half_acc[yh] = expert_term(yh, t)
    for d in range(1, 4):
        near[d - 1].wait_recv()
        idx = lax.rem(yl - d + 4, 4) * 2 + c
        twin.append(send(SL.at[yh, idx], SL.at[yh, idx], sibling))
        half_acc[yh] += expert_term(yh, idx)
    for d in range(4):
        far[d].wait_recv()
        idx = lax.rem(yl - d + 4, 4) * 2 + c
        twin.append(send(SL.at[yo, idx], SL.at[yo, idx], sibling))
        if d == 0:
            half_acc[yo] = expert_term(yo, idx)
        else:
            half_acc[yo] += expert_term(yo, idx)
    for d in range(4):
        twin[d].wait_recv()
        half_acc[yh] += expert_term(yh, lax.rem(yl - d + 4, 4) * 2 + 1 - c)
    for d in range(4):
        twin[4 + d].wait_recv()
        half_acc[yo] += expert_term(yo, lax.rem(yl - d + 4, 4) * 2 + 1 - c)
    for h in range(2):
        for k in range(8):
            acc[k * 40 + h * 20 : k * 40 + h * 20 + 20, :] = half_acc[h, k * 20 : k * 20 + 20, :]
    weights_far.wait()
    WR[yo] = WX[...]
    all_weights = jnp.concatenate(
        [WR[...].reshape(64, 128), jnp.zeros((64, 128), BF16)], axis=0
    )
    slot_weight = jnp.sum(dot_nn(p5[...], all_weights) * m5[...], axis=1, keepdims=True)
    out_h[...] = (slot_weight * acc[...]).astype(BF16)
    products = jnp.sum(hid[...].astype(F32) * acc[...], axis=1, keepdims=True)
    diag = lax.broadcasted_iota(jnp.int32, (40, 128), 0) == lax.broadcasted_iota(
        jnp.int32, (40, 128), 1
    )
    tile = jnp.concatenate(
        [
            jnp.sum(jnp.where(diag, products[k * 40 : (k + 1) * 40], 0.0), axis=0, keepdims=True)
            for k in range(8)
        ],
        axis=0,
    )
    RT0[t] = tile
    own = RT0.at[t]
    ret0 = [send(own, own, t_dev(d)) for d in range(1, 8)]

    tok[3].wait_recv()
    for copy in tok_fwd:
        copy.wait_recv()
    for delta in (0, -1, 1, -2, 2, -3, 3, 4):
        for copy in ax[0, delta]:
            copy.wait_recv()
    for name in ("gate", "up"):
        local[name].wait()
    hd = jnp.zeros((128, 384), F32)
    for k in range(8):
        hd += dot_nn(G[k], W[0, k].reshape(512, 384))
    gate_f = gate[...].astype(F32)
    up_f = up[...].astype(F32)
    sig = jax.nn.sigmoid(gate_f)
    swish = gate_f * sig
    slope = sig * (1.0 + gate_f * (1.0 - sig))
    gd = (hd * up_f * slope).astype(BF16)
    ud = (hd * swish).astype(BF16)

    def sib_copy(zb):
        return pltpu.make_async_remote_copy(
            src_ref=XS.at[zb], dst_ref=XR.at[zb], send_sem=xsend.at[zb], recv_sem=xrecv.at[zb],
            device_id=sibling, device_id_type=MESH,
        )

    def y_copy(zb, src):
        return pltpu.make_async_remote_copy(
            src_ref=YS.at[zb], dst_ref=YR.at[src], send_sem=ysend.at[zb], recv_sem=yrecv.at[src],
            device_id=(e, zb), device_id_type=MESH,
        )

    def part(delta):
        zb = zz(delta)
        for copy in ax[1, delta]:
            copy.wait_recv()
        value = dot_nt(gd, W[1, zb].reshape(512, 384)) + dot_nt(ud, W[2, zb].reshape(512, 384))

        @pl.when(lax.rem(zb, 2) == c)
        def _():
            K[zb] = value

        @pl.when(lax.rem(zb, 2) != c)
        def _():
            XS[zb] = value.astype(BF16)
            sib_copy(zb).start()

    def pass_on(delta):
        zb = zz(delta)

        @pl.when(lax.rem(zb, 2) == c)
        def _():
            sib_copy(zb).wait_recv()
            K[zb] = K[zb] + XR[zb].astype(F32)

            @pl.when(zb != t)
            def _():
                YS[zb] = K[zb].astype(BF16)
                y_copy(zb, yl).start()

    for copy in ret0:
        copy.wait_recv()
    RT1[j] = jnp.sum(RT0[...], axis=0)
    own1 = RT1.at[j]
    ret1 = [send(own1, own1, j_dev(d)) for d in range(1, 8)]
    part(0)
    part(-1)
    pass_on(0)
    part(1)
    pass_on(-1)
    pass_on(1)
    for copy in ret1:
        copy.wait_recv()
    for k in range(8):
        ST2[k] = RT1[:, k, :]
    RT2[z] = ST2[z]
    ret2 = [send(ST2.at[zz(d)], RT2.at[z], z_dev(d)) for d in range(1, 8)]
    part(-2)
    part(2)
    pass_on(-2)
    b_step(1, 3)
    pass_on(2)
    for copy in ret2:
        copy.wait_recv()
    back = RT2[...].reshape(64, 128)
    jf = (j * CAP).astype(F32)
    for k in range(2):
        scores = jnp.dot(
            onehot[k][:, 0:64], back, preferred_element_type=F32, precision=lax.Precision.HIGHEST
        )
        score = jnp.sum(jnp.where(lane == rank[k] + jf, scores, 0.0), axis=1, keepdims=True)
        out_r[k : k + 1, :] = jnp.sum(jnp.where(lane == row, score, 0.0), axis=0, keepdims=True)

    part(-3)
    part(3)
    pass_on(-3)
    b_step(1, 4)
    pass_on(3)
    part(4)
    pass_on(4)
    total = K[t]
    for d in range(1, 4):
        src = lax.rem(yl + d, 4)
        y_copy(t, src).wait_recv()
        total += YR[src].astype(F32)
    out_g[...] = total.astype(BF16)
    for d in range(1, 4):
        y_copy(lax.rem(yl + d, 4) * 2 + c, yl).wait_send()
    for q in range(4):
        sib_copy(q * 2 + 1 - c).wait_send()
    for copy in sends:
        copy.wait_send()


def body(
    grad_out, dense_gate, dense_up, w_gate, w_up, w_down, routes, route_weight,
    expert_down, expert_hidden,
):
    p2, p3, p4, p5, m5 = tables()
    vmem = pl.BlockSpec(memory_space=pltpu.VMEM)
    hbm = pl.BlockSpec(memory_space=pltpu.HBM)
    out_g, out_h, out_r = pl.pallas_call(
        kernel,
        out_shape=(
            jax.ShapeDtypeStruct((128, 512), BF16),
            jax.ShapeDtypeStruct((320, 384), BF16),
            jax.ShapeDtypeStruct((2, 128), F32),
        ),
        in_specs=[vmem] + [hbm] * 14,
        out_specs=(vmem, vmem, vmem),
        scratch_shapes=[
            pltpu.VMEM((128, 384), BF16),
            pltpu.VMEM((128, 384), BF16),
            pltpu.VMEM((2, 128), jnp.int32),
            pltpu.VMEM((320, 384), BF16),
            pltpu.VMEM((8 * BLK, 8 * BLK), BF16),
            pltpu.VMEM((320, 8 * BLK), BF16),
            pltpu.VMEM((64, 8 * BLK), BF16),
            pltpu.VMEM((320, 128), BF16),
            pltpu.VMEM((320, 128), F32),
            pltpu.VMEM((3, 8, 2, 4, 64, 384), BF16),
            pltpu.VMEM((8, 128, 512), BF16),
            pltpu.VMEM((2, 8, 160, 512), BF16),
            pltpu.VMEM((8, BLK, 512), BF16),
            pltpu.VMEM((8, BLK, 512), BF16),
            pltpu.VMEM((4, 96, 512), BF16),
            pltpu.VMEM((4, 96, 512), BF16),
            pltpu.VMEM((2, 160, 512), BF16),
            pltpu.VMEM((2, 32, 128), BF16),
            pltpu.VMEM((32, 128), BF16),
            pltpu.VMEM((384, 4096), BF16),
            pltpu.VMEM((2, 160, 384), F32),
            pltpu.VMEM((320, 384), F32),
            pltpu.VMEM((8, 128, 512), F32),
            pltpu.VMEM((8, 128, 512), BF16),
            pltpu.VMEM((8, 128, 512), BF16),
            pltpu.VMEM((8, 128, 512), BF16),
            pltpu.VMEM((4, 128, 512), BF16),
            pltpu.VMEM((8, 8, 128), F32),
            pltpu.VMEM((8, 8, 128), F32),
            pltpu.VMEM((8, 8, 128), F32),
            pltpu.VMEM((8, 8, 128), F32),
            pltpu.SemaphoreType.DMA((N_COPY,)),
            pltpu.SemaphoreType.DMA((N_COPY,)),
            pltpu.SemaphoreType.DMA((16,)),
            pltpu.SemaphoreType.DMA((8,)),
            pltpu.SemaphoreType.DMA((8,)),
            pltpu.SemaphoreType.DMA((8,)),
            pltpu.SemaphoreType.DMA((4,)),
        ],
        compiler_params=pltpu.CompilerParams(
            collective_id=0, has_side_effects=True, vmem_limit_bytes=60 << 20
        ),
    )(
        route_weight.T, grad_out, dense_gate, dense_up, w_down.T, w_gate, w_up, routes.T,
        expert_down[0], expert_hidden[0],
        jnp.asarray(p2, BF16), jnp.asarray(p3, BF16), jnp.asarray(p4, BF16), jnp.asarray(p5, BF16),
        jnp.asarray(m5, F32),
    )
    return out_g, out_h[None], out_r.T


def solution(mesh):
    in_specs = (
        P("expert", "tensor"),
        P("expert", "tensor"),
        P("expert", "tensor"),
        P("expert", "tensor"),
        P("expert", "tensor"),
        P("tensor", "expert"),
        P("expert", None),
        P("expert", None),
        P("expert", "tensor", None),
        P("expert", None, "tensor"),
    )
    out_specs = (P("expert", "tensor"), P("expert", None, "tensor"), P("expert", None))
    return jax.shard_map(body, mesh=mesh, in_specs=in_specs, out_specs=out_specs, check_vma=False)
```

time: 131 us -> 118 us (0.901)
  the two profiles are of different devices: /device:TPU:48 before, /device:TPU:80 now
where the time goes in v2:
time: 118 us
  Pallas kernels  112 us (95%)
  local copies, waits for them, and re-layouts  4.46 us (4%)
    pallas_call x1, Pallas kernels, body(): pl.pallas_call(kernel, out_shape=(jax.ShapeDtypeStruct((128, 512), BF16),...  112 us
    unnamed x3, local copies, waits for them, and re-layouts  4.46 us

profile of v2, /device:TPU:80, one launch (start us, length us, event | category | flops | bytes accessed | tf_op | source)
XLA Modules:
  0.0 117.6 jit_solution(11858857774363956235)
XLA Ops:
  0.6 112.5 %shard_map.166 = (bf16[128,512]{1,0:T(8,128)(2,1)}, bf16[320,384]{1,0:T(8,128)(2,1)}, f32[2,128]{1,0:T(2,128)}) custom-call(bf16[2,128]{1,0:T(2,128)(2,1)} %bitcast.13, bf16[128,512]{1,0:T(8,128)(2,1)} %grad_in.1, bf16[128,384]{1,0:T(8,128)(2,1)} %gate_in.1, bf16[128,384]{1,0:T(8,128)(2,1)} %up_in.1, bf16[64,384]{1,0:T(8,128)(2,1)} %bitcast.10, ...), custom_call_target="tpu_custom_call" | custom-call | tf_op jit(solution)/shard_map/pallas_call | solution.py:466
  113.1 1.6 %copy.21 = bf16[128,512]{1,0:T(8,128)(2,1)} copy(bf16[128,512]{1,0:T(8,128)(2,1)} %get-tuple-element.12) | data formatting | bytes 262144
  114.7 1.7 %copy.22 = bf16[1,320,384]{2,1,0:T(8,128)(2,1)} copy(bf16[1,320,384]{2,1,0:T(8,128)(2,1)} %bitcast.9) | data formatting | bytes 491520
  116.4 1.2 %copy.23 = f32[128,2]{0,1:T(2,128)} copy(f32[128,2]{0,1:T(2,128)} %bitcast.11) | data formatting | bytes 2048

commit v3 on v2

--- a/solution.py
+++ b/solution.py
@@ -11,7 +11,7 @@
 BF16 = jnp.bfloat16
 CAP = 5
 BLK = 48
-N_COPY = 160
+N_COPY = 224
 
 
 def dot_nt(a, b):
@@ -137,22 +137,36 @@
 
     kinds = (pl.ds(0, 1), pl.ds(1, 2))
 
-    def ring(kd, half, step, right):
+    def ring(key, step, right):
         sign = 1 if right else -1
         zc = zz(-sign * (step - 1))
-        if half == "own":
-            ref = W.at[kinds[kd], zc, yh]
+        if key == "own":
+            ref = W.at[kinds[1], zc, yh]
             if step == 4:
-                ref = W.at[kinds[kd], zc, yh, pl.ds(0 if right else 2, 2)]
+                ref = W.at[kinds[1], zc, yh, pl.ds(0 if right else 2, 2)]
         else:
-            ref = W.at[kinds[kd], zc, yo, x]
+            kd, far_half = key
+            half = yo if far_half else yh
+            ref = W.at[kinds[kd], zc, half, x]
             if step == 4:
-                ref = W.at[kinds[kd], zc, yo, x, pl.ds(0 if right else 32, 32)]
+                ref = W.at[kinds[kd], zc, half, x, pl.ds(0 if right else 32, 32)]
         return send(ref, ref, z_dev(sign))
 
-    def x_send(kd, delta, half):
-        ref = W.at[kinds[kd], zz(delta), half, x]
-        return [send(ref, ref, x_dev(d)) for d in range(1, 4)]
+    def x_send(key, delta):
+        kd, far_half = key
+        ref = W.at[kinds[kd], zz(delta), yo if far_half else yh, x]
+        return [send(ref, ref, x_dev(1)), send(ref, ref, x_dev(3))]
+
+    def x_relay(key, delta):
+        kd, far_half = key
+        block = W.at[kinds[kd], zz(delta), yo if far_half else yh]
+        ax[key, delta][0].wait_recv()
+        low = block.at[:, xx(3), pl.ds(0, 32)]
+        relay = [send(low, low, x_dev(1))]
+        ax[key, delta][1].wait_recv()
+        high = block.at[:, xx(1), pl.ds(32, 32)]
+        relay.append(send(high, high, x_dev(3)))
+        ar[key, delta] = relay
 
     def gather_start(buf):
         own = buf.at[t]
@@ -169,39 +183,48 @@
     a = {}
     b = {}
     ax = {}
-    bx = {}
-
-    def a_open(kd):
-        across[kd].wait_recv()
+    ar = {}
+    down_own, down_far, wide_far = (0, False), (0, True), (1, True)
+
+    def a_open(key):
+        if key[1]:
+            across[key[0]].wait_recv()
         for right in (True, False):
-            a[kd, 1, right] = ring(kd, "other", 1, right)
-        ax[kd, 0] = x_send(kd, 0, yo)
-
-    def a_step(kd, step):
-        a[kd, step, True].wait_recv()
+            a[key, 1, right] = ring(key, 1, right)
+        ax[key, 0] = x_send(key, 0)
+
+    def a_step(key, step):
+        a[key, step, True].wait_recv()
         if step < 4:
-            a[kd, step + 1, True] = ring(kd, "other", step + 1, True)
-        a[kd, step, False].wait_recv()
+            a[key, step + 1, True] = ring(key, step + 1, True)
+        a[key, step, False].wait_recv()
         if step < 4:
-            a[kd, step + 1, False] = ring(kd, "other", step + 1, False)
-            ax[kd, -step] = x_send(kd, -step, yo)
-            ax[kd, step] = x_send(kd, step, yo)
+            a[key, step + 1, False] = ring(key, step + 1, False)
+            ax[key, -step] = x_send(key, -step)
+            ax[key, step] = x_send(key, step)
         else:
-            ax[kd, 4] = x_send(kd, 4, yo)
-
-    def b_open(kd):
-        for copy in bx[kd]:
+            ax[key, 4] = x_send(key, 4)
+
+    def relay_step(key, step):
+        if step in (0, 4):
+            x_relay(key, step)
+        else:
+            x_relay(key, -step)
+            x_relay(key, step)
+
+    def b_open():
+        for copy in bx:
             copy.wait_recv()
         for right in (True, False):
-            b[kd, 1, right] = ring(kd, "own", 1, right)
-
-    def b_step(kd, step):
-        b[kd, step, True].wait_recv()
+            b[1, right] = ring("own", 1, right)
+
+    def b_step(step):
+        b[step, True].wait_recv()
         if step < 4:
-            b[kd, step + 1, True] = ring(kd, "own", step + 1, True)
-        b[kd, step, False].wait_recv()
+            b[step + 1, True] = ring("own", step + 1, True)
+        b[step, False].wait_recv()
         if step < 4:
-            b[kd, step + 1, False] = ring(kd, "own", step + 1, False)
+            b[step + 1, False] = ring("own", step + 1, False)
 
     lane = lax.broadcasted_iota(jnp.int32, (128, 128), 1).astype(F32)
     row = lax.broadcasted_iota(jnp.int32, (128, 128), 0).astype(F32)
@@ -238,15 +261,17 @@
     R1[z] = S1[z]
 
     pl.semaphore_wait(barrier, 24)
-    disp1 = [send(S1.at[zz(d)], R1.at[z], z_dev(d)) for d in range(1, 8)]
     local["wd"].wait()
     local["wg"].wait()
     local["wu"].wait()
-    across = {}
+    a_open(down_own)
+    ref = W.at[kinds[1], z, yh, x]
+    bx = [send(ref, ref, x_dev(d)) for d in range(1, 4)]
+    across = []
     for kd in range(2):
         ref = W.at[kinds[kd], z, yh, x]
-        bx[kd] = x_send(kd, 0, yh)
-        across[kd] = send(ref, ref, y_dev)
+        across.append(send(ref, ref, y_dev))
+    disp1 = [send(S1.at[zz(d)], R1.at[z], z_dev(d)) for d in range(1, 8)]
     tok = gather_start(G)
     local["p2"].wait()
     for copy in disp1:
@@ -255,16 +280,13 @@
     S2[...] = shuffled.reshape(4, 96, 512)
     R2[x] = S2[x]
     disp2 = [send(S2.at[xx(d)], R2.at[x], x_dev(d)) for d in range(1, 4)]
-    b_open(0)
-    b_open(1)
-
-    a_open(0)
-    b_step(0, 1)
-    a_open(1)
-    a_step(0, 1)
+    a_step(down_own, 1)
+    b_open()
+    a_open(down_far)
+    a_open(wide_far)
+    a_step(down_own, 2)
     tok_fwd = gather_forward(G, tok)
 
-    a_step(1, 1)
     for name in ("p3", "p4", "p5", "m5"):
         local[name].wait()
     for copy in disp2:
@@ -280,17 +302,32 @@
     weights_far = send(WR.at[yo], WX, y_dev)
     sends.pop()
 
-    b_step(0, 2)
-    a_step(0, 2)
-    b_step(1, 1)
-    a_step(1, 2)
-    b_step(0, 3)
-    a_step(0, 3)
-    a_step(1, 3)
-    a_step(0, 4)
-    b_step(0, 4)
-    a_step(1, 4)
-    b_step(1, 2)
+    a_step(down_far, 1)
+    a_step(wide_far, 1)
+    a_step(down_own, 3)
+    a_step(down_far, 2)
+    a_step(down_own, 4)
+    relay_step(down_own, 0)
+    b_step(1)
+    a_step(wide_far, 2)
+    relay_step(down_own, 1)
+    relay_step(down_far, 0)
+    a_step(down_far, 3)
+    relay_step(wide_far, 0)
+    relay_step(down_own, 2)
+    relay_step(down_far, 1)
+    a_step(wide_far, 3)
+    a_step(down_far, 4)
+    b_step(2)
+    relay_step(down_own, 3)
+    relay_step(wide_far, 1)
+    relay_step(down_far, 2)
+    a_step(wide_far, 4)
+    relay_step(down_own, 4)
+    relay_step(down_far, 3)
+    relay_step(wide_far, 2)
+    relay_step(down_far, 4)
+    relay_step(wide_far, 3)
 
     for name in ("hid", "ed"):
         local[name].wait()
@@ -343,11 +380,13 @@
     own = RT0.at[t]
     ret0 = [send(own, own, t_dev(d)) for d in range(1, 8)]
 
+    b_step(3)
+
     tok[3].wait_recv()
     for copy in tok_fwd:
         copy.wait_recv()
     for delta in (0, -1, 1, -2, 2, -3, 3, 4):
-        for copy in ax[0, delta]:
+        for copy in ar[down_own, delta] + ar[down_far, delta]:
             copy.wait_recv()
     for name in ("gate", "up"):
         local[name].wait()
@@ -376,7 +415,7 @@
 
     def part(delta):
         zb = zz(delta)
-        for copy in ax[1, delta]:
+        for copy in ar[wide_far, delta]:
             copy.wait_recv()
         value = dot_nt(gd, W[1, zb].reshape(512, 384)) + dot_nt(ud, W[2, zb].reshape(512, 384))
 
@@ -422,7 +461,6 @@
     part(-2)
     part(2)
     pass_on(-2)
-    b_step(1, 3)
     pass_on(2)
     for copy in ret2:
         copy.wait_recv()
@@ -438,7 +476,8 @@
     part(-3)
     part(3)
     pass_on(-3)
-    b_step(1, 4)
+    x_relay(wide_far, 4)
+    b_step(4)
     pass_on(3)
     part(4)
     pass_on(4)

time: 118 us -> 114 us (0.966)
  the two profiles are of different devices: /device:TPU:80 before, /device:TPU:16 now
where the time goes in v3:
time: 114 us
  Pallas kernels  109 us (96%)
  local copies, waits for them, and re-layouts  4.46 us (4%)
    pallas_call x1, Pallas kernels, body(): pl.pallas_call(kernel, out_shape=(jax.ShapeDtypeStruct((128, 512), BF16),...  109 us
    unnamed x3, local copies, waits for them, and re-layouts  4.46 us

profile of v3, /device:TPU:16, one launch (start us, length us, event | category | flops | bytes accessed | tf_op | source)
XLA Modules:
  0.0 113.9 jit_solution(5945694904994247253)
XLA Ops:
  0.6 108.8 %shard_map.166 = (bf16[128,512]{1,0:T(8,128)(2,1)}, bf16[320,384]{1,0:T(8,128)(2,1)}, f32[2,128]{1,0:T(2,128)}) custom-call(bf16[2,128]{1,0:T(2,128)(2,1)} %bitcast.13, bf16[128,512]{1,0:T(8,128)(2,1)} %grad_in.1, bf16[128,384]{1,0:T(8,128)(2,1)} %gate_in.1, bf16[128,384]{1,0:T(8,128)(2,1)} %up_in.1, bf16[64,384]{1,0:T(8,128)(2,1)} %bitcast.10, ...), custom_call_target="tpu_custom_call" | custom-call | tf_op jit(solution)/shard_map/pallas_call | solution.py:505
  109.5 1.6 %copy.21 = bf16[128,512]{1,0:T(8,128)(2,1)} copy(bf16[128,512]{1,0:T(8,128)(2,1)} %get-tuple-element.12) | data formatting | bytes 262144
  111.0 1.7 %copy.22 = bf16[1,320,384]{2,1,0:T(8,128)(2,1)} copy(bf16[1,320,384]{2,1,0:T(8,128)(2,1)} %bitcast.9) | data formatting | bytes 491520
  112.7 1.2 %copy.23 = f32[128,2]{0,1:T(2,128)} copy(f32[128,2]{0,1:T(2,128)} %bitcast.11) | data formatting | bytes 2048

commit v4 on v3

--- a/solution.py
+++ b/solution.py
@@ -323,12 +323,6 @@
     relay_step(wide_far, 1)
     relay_step(down_far, 2)
     a_step(wide_far, 4)
-    relay_step(down_own, 4)
-    relay_step(down_far, 3)
-    relay_step(wide_far, 2)
-    relay_step(down_far, 4)
-    relay_step(wide_far, 3)
-
     for name in ("hid", "ed"):
         local[name].wait()
     def expert_term(h, idx):
@@ -380,6 +374,23 @@
     own = RT0.at[t]
     ret0 = [send(own, own, t_dev(d)) for d in range(1, 8)]
 
+    relay_step(down_own, 4)
+    relay_step(down_far, 3)
+    for copy in ret0:
+        copy.wait_recv()
+    RT1[j] = jnp.sum(RT0[...], axis=0)
+    own1 = RT1.at[j]
+    ret1 = [send(own1, own1, j_dev(d)) for d in range(1, 8)]
+    relay_step(wide_far, 2)
+    relay_step(down_far, 4)
+    relay_step(wide_far, 3)
+    for copy in ret1:
+        copy.wait_recv()
+    for k in range(8):
+        ST2[k] = RT1[:, k, :]
+    RT2[z] = ST2[z]
+    ret2 = [send(ST2.at[zz(d)], RT2.at[z], z_dev(d)) for d in range(1, 8)]
+    x_relay(wide_far, 4)
     b_step(3)
 
     tok[3].wait_recv()
@@ -441,23 +452,12 @@
                 YS[zb] = K[zb].astype(BF16)
                 y_copy(zb, yl).start()
 
-    for copy in ret0:
-        copy.wait_recv()
-    RT1[j] = jnp.sum(RT0[...], axis=0)
-    own1 = RT1.at[j]
-    ret1 = [send(own1, own1, j_dev(d)) for d in range(1, 8)]
     part(0)
     part(-1)
     pass_on(0)
     part(1)
     pass_on(-1)
     pass_on(1)
-    for copy in ret1:
-        copy.wait_recv()
-    for k in range(8):
-        ST2[k] = RT1[:, k, :]
-    RT2[z] = ST2[z]
-    ret2 = [send(ST2.at[zz(d)], RT2.at[z], z_dev(d)) for d in range(1, 8)]
     part(-2)
     part(2)
     pass_on(-2)
@@ -476,7 +476,6 @@
     part(-3)
     part(3)
     pass_on(-3)
-    x_relay(wide_far, 4)
     b_step(4)
     pass_on(3)
     part(4)

time: 114 us -> 109 us (0.956)
  the two profiles are of different devices: /device:TPU:16 before, /device:TPU:80 now
where the time goes in v4:
time: 109 us
  Pallas kernels  104 us (95%)
  local copies, waits for them, and re-layouts  4.46 us (4%)
    pallas_call x1, Pallas kernels, body(): pl.pallas_call(kernel, out_shape=(jax.ShapeDtypeStruct((128, 512), BF16),...  104 us
    unnamed x3, local copies, waits for them, and re-layouts  4.46 us

profile of v4, /device:TPU:80, one launch (start us, length us, event | category | flops | bytes accessed | tf_op | source)
XLA Modules:
  0.0 109.0 jit_solution(5495040605501012619)
XLA Ops:
  0.6 103.9 %shard_map.166 = (bf16[128,512]{1,0:T(8,128)(2,1)}, bf16[320,384]{1,0:T(8,128)(2,1)}, f32[2,128]{1,0:T(2,128)}) custom-call(bf16[2,128]{1,0:T(2,128)(2,1)} %bitcast.13, bf16[128,512]{1,0:T(8,128)(2,1)} %grad_in.1, bf16[128,384]{1,0:T(8,128)(2,1)} %gate_in.1, bf16[128,384]{1,0:T(8,128)(2,1)} %up_in.1, bf16[64,384]{1,0:T(8,128)(2,1)} %bitcast.10, ...), custom_call_target="tpu_custom_call" | custom-call | tf_op jit(solution)/shard_map/pallas_call | solution.py:504
  104.5 1.6 %copy.21 = bf16[128,512]{1,0:T(8,128)(2,1)} copy(bf16[128,512]{1,0:T(8,128)(2,1)} %get-tuple-element.12) | data formatting | bytes 262144
  106.1 1.7 %copy.22 = bf16[1,320,384]{2,1,0:T(8,128)(2,1)} copy(bf16[1,320,384]{2,1,0:T(8,128)(2,1)} %bitcast.9) | data formatting | bytes 491520
  107.7 1.2 %copy.23 = f32[128,2]{0,1:T(2,128)} copy(f32[128,2]{0,1:T(2,128)} %bitcast.11) | data formatting | bytes 2048

commit v5 on v4

--- a/solution.py
+++ b/solution.py
@@ -322,7 +322,7 @@
     relay_step(down_own, 3)
     relay_step(wide_far, 1)
     relay_step(down_far, 2)
-    a_step(wide_far, 4)
+
     for name in ("hid", "ed"):
         local[name].wait()
     def expert_term(h, idx):
@@ -373,6 +373,8 @@
     RT0[t] = tile
     own = RT0.at[t]
     ret0 = [send(own, own, t_dev(d)) for d in range(1, 8)]
+
+    a_step(wide_far, 4)
 
     relay_step(down_own, 4)
     relay_step(down_far, 3)

time: 109 us -> 109 us (level)
  no operation moved by 1% of the time
where the time goes in v5:
time: 109 us
  Pallas kernels  104 us (95%)
  local copies, waits for them, and re-layouts  4.46 us (4%)
    pallas_call x1, Pallas kernels, body(): pl.pallas_call(kernel, out_shape=(jax.ShapeDtypeStruct((128, 512), BF16),...  104 us
    unnamed x3, local copies, waits for them, and re-layouts  4.46 us

profile of v5, /device:TPU:80, one launch (start us, length us, event | category | flops | bytes accessed | tf_op | source)
XLA Modules:
  0.0 109.0 jit_solution(7370126284840110265)
XLA Ops:
  0.6 103.9 %shard_map.166 = (bf16[128,512]{1,0:T(8,128)(2,1)}, bf16[320,384]{1,0:T(8,128)(2,1)}, f32[2,128]{1,0:T(2,128)}) custom-call(bf16[2,128]{1,0:T(2,128)(2,1)} %bitcast.13, bf16[128,512]{1,0:T(8,128)(2,1)} %grad_in.1, bf16[128,384]{1,0:T(8,128)(2,1)} %gate_in.1, bf16[128,384]{1,0:T(8,128)(2,1)} %up_in.1, bf16[64,384]{1,0:T(8,128)(2,1)} %bitcast.10, ...), custom_call_target="tpu_custom_call" | custom-call | tf_op jit(solution)/shard_map/pallas_call | solution.py:506
  104.5 1.6 %copy.21 = bf16[128,512]{1,0:T(8,128)(2,1)} copy(bf16[128,512]{1,0:T(8,128)(2,1)} %get-tuple-element.12) | data formatting | bytes 262144
  106.1 1.7 %copy.22 = bf16[1,320,384]{2,1,0:T(8,128)(2,1)} copy(bf16[1,320,384]{2,1,0:T(8,128)(2,1)} %bitcast.9) | data formatting | bytes 491520
  107.7 1.2 %copy.23 = f32[128,2]{0,1:T(2,128)} copy(f32[128,2]{0,1:T(2,128)} %bitcast.11) | data formatting | bytes 2048
